TPU v7x, 32 devices: a whole 2x2x4 slice. The times are simulated.
32 devices in a mesh: ctx: 16 (over z, x, core), head: 2 (over y).
Axes of the slice: x: 2, y: 2, z: 4, core: 2. Of those that a mesh axis runs over, the one named last changes fastest.
Arguments:
- kv_latent: bfloat16 [8192, 576], P('ctx'), may hold values from -4 to 4
- queries: bfloat16 [8192, 3072], P('ctx', 'head'), may hold values from -22 to 22
- grad_out: bfloat16 [8192, 2048], P('ctx', 'head'), may hold values from -6 to 6
- kv_up_weight: bfloat16 [512, 4096], P(None, 'head'), may hold values from -0.25 to 0.25
- doc_ids: int32 [8192], replicated, may hold values from 0 to 7, never falling along the last dimension, each value on 1 to 1536 neighbouring positions
Outputs:
- grad_queries: bfloat16 [8192, 3072], P('ctx', 'head')
- grad_latent: bfloat16 [8192, 576], P('ctx')
- grad_weight: float32 [512, 4096], P('ctx', 'head')
Inputs may be any that keep to these rules, and one draw needn't show every extreme that they name: `doc_ids`: document ids never fall along the sequence; every document has 1 to 1536 tokens, and one has exactly 1536.
All inputs are finite; a program needn't handle non-finite values.
Results may differ from a plain program's by a relative error of at most 0.0076.
Values may be sent and summed in bfloat16 or wider, within the bound.
No kernel may reach another device: no remote copies, remote signals or barrier semaphores. Data moves between devices by JAX's collectives and lax.ppermute only.
A program may use at most 128 MiB of HBM per device.

v0:
```python
import functools
import math

import jax
import jax.numpy as jnp
from jax import lax
from jax.experimental import pallas as pl
from jax.experimental.pallas import tpu as pltpu
from jax.sharding import PartitionSpec as P

NOPE = 128
ROPE = 64
VDIM = 128
LATENT = 512
REACH = 3
QK = NOPE + ROPE
KV = NOPE + VDIM
WIDTH = LATENT + ROPE
LANES = 128

MASKED = -1e30
FLOOR = -1e20
SCALE = 1.0 / math.sqrt(QK)
SCALE2 = SCALE * math.log2(math.e)

NT = (((1,), (1,)), ((), ()))
NN = (((1,), (0,)), ((), ()))


def dot(a, b, dims=NN):
    return lax.dot_general(a, b, dims, preferred_element_type=jnp.float32)


def head_cols(h, size):
    return slice(h * size, (h + 1) * size)


def fold(value, combine):
    return combine(value.reshape(-1, 8, value.shape[1]), axis=0)


def fold(value, combine):
    return combine(value.reshape(-1, 8, value.shape[1]), axis=0)


def lift(latent, w_ref, k_out, v_out):
    for h in range(w_ref.shape[1] // KV):
        lifted = dot(latent[:, :LATENT], w_ref[:, head_cols(h, KV)]).astype(jnp.bfloat16)
        k_out(h, jnp.concatenate([lifted[:, :NOPE], latent[:, LATENT:]], axis=1))
        v_out(h, lifted[:, NOPE:])


def score_block(key, value, q_ref, do_ref, bounds, run_ref, raw_ref, graw_ref, keep):
    rows = do_ref.shape[0]
    heads = range(do_ref.shape[1] // VDIM)
    lower, upper = bounds
    for h in heads:
        raw_ref[h] = dot(key(h), q_ref[:, head_cols(h, QK)], NT)
        graw_ref[h] = dot(value(h), do_ref[:, head_cols(h, VDIM)], NT)
    index = lax.broadcasted_iota(jnp.int32, (LANES, LANES), 0)
    pieces = [slice(r, r + LANES) for r in range(0, rows, LANES)]
    for h in heads:
        for c in range(0, rows, LANES):
            cols = slice(c, c + LANES)

            def scores(part):
                place = index + part.start
                seen = (place >= lower[:, cols]) & (place <= upper[:, cols])
                return jnp.where(seen, raw_ref[h, part, cols] * SCALE2, MASKED)

            high = None
            for part in pieces:
                piece = fold(scores(part), jnp.max)
                high = piece if high is None else jnp.maximum(high, piece)
            old_top = run_ref[h, 0:1, cols]
            new_top = jnp.maximum(old_top, jnp.max(high, axis=0, keepdims=True))
            mass, cross = 0.0, 0.0
            for part in pieces:
                weights = jnp.exp2(scores(part) - new_top)
                grads = graw_ref[h, part, cols]
                keep(h, part, cols, weights.astype(jnp.bfloat16), grads.astype(jnp.bfloat16))
                mass = mass + fold(weights, jnp.sum)
                cross = cross + fold(weights * grads, jnp.sum)
            factor = jnp.exp2(old_top - new_top)
            run_ref[h, 0:1, cols] = new_top
            run_ref[h, 1:2, cols] = run_ref[h, 1:2, cols] * factor + jnp.sum(
                mass, axis=0, keepdims=True
            )
            run_ref[h, 2:3, cols] = run_ref[h, 2:3, cols] * factor + jnp.sum(
                cross, axis=0, keepdims=True
            )


def grad_block(kept, key, top, end_ref, q_t, do_t, low_ref, ds_ref, dq_acc, d_acc, r_add):
    rows = do_t.shape[1]
    heads = range(do_t.shape[0] // VDIM)
    for h in heads:
        factor = jnp.exp2(top(h) - end_ref[h, 0:1, :]) * end_ref[h, 1:2, :]
        delta = end_ref[h, 2:3, :]
        for c in range(0, rows, LANES):
            cols = slice(c, c + LANES)
            for r in range(0, rows, LANES):
                part = slice(r, r + LANES)
                weights, grads = kept(h, part, cols)
                probs = weights.astype(jnp.float32) * factor[:, cols]
                low_ref[h, part, cols] = probs.astype(jnp.bfloat16)
                ds_ref[h, part, cols] = (
                    probs * (grads.astype(jnp.float32) - delta[:, cols])
                ).astype(jnp.bfloat16)
    rope = 0.0
    for h in heads:
        dvalue = dot(do_t[head_cols(h, VDIM), :], low_ref[h], NT)
        dkey = dot(q_t[head_cols(h, QK), :], ds_ref[h], NT) * SCALE
        dq_acc[head_cols(h, QK), :] += dot(key(h).T, ds_ref[h])
        d_acc[h * KV : h * KV + NOPE, :] += dkey[:NOPE]
        d_acc[h * KV + NOPE : (h + 1) * KV, :] += dvalue
        rope = rope + dkey[NOPE:]
    r_add(rope)


def start_stats(run_ref):
    count, rows = run_ref.shape[0], run_ref.shape[2]
    for h in range(count):
        run_ref[h, 0:1, :] = jnp.full((1, rows), FLOOR, jnp.float32)
        run_ref[h, 1:8, :] = jnp.zeros((7, rows), jnp.float32)


def chip_place(index_ref):
    core = lax.rem(index_ref[0], 2)
    return core, index_ref[0] - core


def order_pair(out_ref, core, own, other):
    out_ref[core] = own[...]
    out_ref[1 - core] = other[...]


LOCAL = ((1, REACH), (0, REACH), (1, REACH + 1))


def query_bounds(start_ref, chip, j, t, rows):
    lower = start_ref[j, 0:1, :] - (chip + t - REACH) * rows
    upper = lax.broadcasted_iota(jnp.int32, (1, rows), 1) + (j + REACH - t) * rows
    return lower, upper


def find_starts(docs_ref, start_ref, chip, rows):
    for j in range(2):
        block = chip + j
        my_docs = docs_ref[:, pl.ds(pl.multiple_of(block * rows, rows), rows)]
        first_doc = my_docs[:, :1]
        key_docs = jnp.broadcast_to(my_docs, (128, rows)).T[:, :1]
        inside = jnp.sum(jnp.where(key_docs < my_docs, 1.0, 0.0), axis=0, keepdims=True)
        before = jnp.zeros((1, rows), jnp.float32)
        for back in range(1, REACH + 1):
            earlier = jnp.maximum(block - back, 0)
            docs = docs_ref[:, pl.ds(pl.multiple_of(earlier * rows, rows), rows)]
            same = (docs == first_doc) & (block >= back)
            before = before + jnp.where(same, 1.0, 0.0)
        before = jnp.sum(before, axis=1, keepdims=True)
        start = jnp.where(my_docs == first_doc, -before, inside).astype(jnp.int32)
        start_ref[j, 0:1, :] = start + block * rows


def local_kernel(
    index_ref, docs_ref, q0, do0, q1, do1, w_ref, lat0, lat1,
    e_ref, g_ref, k_ref, run_ref, top_ref, start_ref,
    q_ref, do_ref, lat_ref, v_ref, raw_ref, graw_ref,
):
    rows = q0.shape[0]
    core, chip = chip_place(index_ref)
    heads = w_ref.shape[1] // KV

    @pl.when(pl.program_id(0) == 0)
    def _():
        lat_ref[core] = lat0[...].T
        lat_ref[1 - core] = lat1[...].T
        find_starts(docs_ref, start_ref, chip, rows)

    order_pair(q_ref, core, q0, q1)
    order_pair(do_ref, core, do0, do1)
    for j in range(2):

        def k_out(h, key):
            k_ref[0, j * heads + h] = key

        def v_out(h, value):
            v_ref[j * heads + h] = value

        lift(lat_ref[j], w_ref, k_out, v_out)
        start_stats(run_ref.at[0, pl.ds(j * heads, heads)])
    for n, (j, t) in enumerate(LOCAL):
        slot = t - REACH

        def keep(h, part, cols, weights, grads):
            e_ref[0, n * heads + h, part, cols] = weights
            g_ref[0, n * heads + h, part, cols] = grads

        run = run_ref.at[0, pl.ds(j * heads, heads)]
        score_block(
            lambda h: k_ref[0, slot * heads + h], lambda h: v_ref[slot * heads + h],
            q_ref.at[j], do_ref.at[j], query_bounds(start_ref, chip, j, t, rows), run,
            raw_ref, graw_ref, keep,
        )
        for h in range(heads):
            top_ref[0, n * heads + h] = run[h]


def main_kernel(ranks, steps, index_ref, docs_sref, q0, do0, q1, do1, w_ref, *refs):
    kept, refs = [refs[5 * n : 5 * n + 5] for n in range(steps)], refs[5 * steps :]
    main_body(ranks, index_ref, docs_sref, q0, do0, q1, do1, w_ref, kept, *refs)


def main_body(
    ranks, index_ref, docs_sref, q0, do0, q1, do1, w_ref, kept_steps, start_ref,
    lat_far, lat_swap, lat_mixed, lat_passed, lat_own, lat_other,
    dq0_ref, dq1_ref, keep_ref, send_ref, x_old, x_far, x_swap, x_own, x_other,
    q_ref, do_ref, lat_ref, lat_t_ref, e_ref, g_ref, k_ref, v_ref, top_ref,
    run_ref, end_ref, raw_ref, graw_ref, low_ref, ds_ref, dq_acc, d_acc, gw_acc, x_acc,
    local_e, local_g, local_k, local_run, local_top, sems, kept_sems,
):
    step = pl.program_id(0)
    rows = q0.shape[0]
    heads = w_ref.shape[1] // KV
    blocks = REACH + 2

    kept_copies = []
    for n, (all_e, all_g, all_k, all_run, all_top) in enumerate(kept_steps):
        copies = [
            pltpu.make_async_copy(all_e.at[0], local_e, kept_sems.at[0]),
            pltpu.make_async_copy(all_g.at[0], local_g, kept_sems.at[1]),
        ]
        kept_copies = kept_copies or copies

        @pl.when(step == n)
        def _():
            for copy in copies:
                copy.start()
            local_k[...] = all_k[0]
            local_run[...] = all_run[0]
            local_top[...] = all_top[0]

    core, chip = chip_place(index_ref)

    def active(j, t):
        block = chip + t - REACH
        last_doc = docs_sref[jnp.maximum(block, 0) * rows + rows - 1]
        return (block >= 0) & (last_doc >= docs_sref[(chip + j) * rows])

    def block_rows(t):
        return pl.ds(pl.multiple_of(t * rows, rows), rows)

    def piece_rows(t, part):
        size = part.stop - part.start
        return pl.ds(pl.multiple_of(t * rows + part.start, size), size)

    def loop(first, last, when, body):
        def visit(t, carry):
            @pl.when(when(t))
            def _():
                body(t)

            return carry

        lax.fori_loop(first, last, visit, 0)

    @pl.when(step == 0)
    def _():
        places = [(lat_far, 1 + core), (lat_swap, 2 - core), (lat_own, REACH + core),
                  (lat_other, REACH + 1 - core)]
        copies = [
            pltpu.make_async_copy(source, lat_t_ref.at[:, block_rows(t)], sems.at[i])
            for i, (source, t) in enumerate(places)
        ]
        first = lat_t_ref.at[:, block_rows(0)]
        oldest = pltpu.make_async_copy(lat_mixed, first, sems.at[4])
        passed = pltpu.make_async_copy(lat_passed, first, sems.at[4])
        for copy in copies:
            copy.start()
        pl.when(core == 0)(oldest.start)
        pl.when(core == 1)(passed.start)
        x_acc[...] = jnp.zeros_like(x_acc)
        for copy in copies:
            copy.wait()
        oldest.wait()
        for t in range(REACH):
            part = slice(t * rows, (t + 1) * rows)
            lat_ref[part, :] = lat_t_ref[:, part].T

    order_pair(q_ref, core, q0, q1)
    order_pair(do_ref, core, do0, do1)
    gw_acc[...] = jnp.zeros_like(gw_acc)
    dq_acc[...] = jnp.zeros_like(dq_acc)
    d_acc[...] = jnp.zeros_like(d_acc)

    def lift_block(t):
        def k_out(h, key):
            k_ref[h, block_rows(t), :] = key

        def v_out(h, value):
            v_ref[h, block_rows(t), :] = value

        lift(lat_ref[block_rows(t), :], w_ref, k_out, v_out)

    loop(0, REACH, lambda t: active(0, t) | active(1, t), lift_block)

    for j in range(2):
        for h in range(heads):
            run_ref[h] = local_run[j * heads + h]

        def first_pass(t):
            def keep(h, part, cols, weights, grads):
                e_ref[h, piece_rows(t, part), cols] = weights
                g_ref[h, piece_rows(t, part), cols] = grads

            score_block(
                lambda h: k_ref[h, block_rows(t), :], lambda h: v_ref[h, block_rows(t), :],
                q_ref.at[j], do_ref.at[j], query_bounds(start_ref, chip, j, t, rows), run_ref,
                raw_ref, graw_ref, keep,
            )
            for h in range(heads):
                top_ref[h, t] = run_ref[h]

        loop(j, REACH, lambda t: active(j, t), first_pass)
        for h in range(heads):
            inverse = 1.0 / run_ref[h, 1:2, :]
            end_ref[h, 0:1, :] = run_ref[h, 0:1, :]
            end_ref[h, 1:2, :] = inverse
            end_ref[h, 2:3, :] = run_ref[h, 2:3, :] * inverse
        q_t, do_t = q_ref[j].T, do_ref[j].T

        def add(t, part, kept, key, top):
            def r_add(rope):
                x_acc[LATENT:, part] += rope

            grad_block(
                kept, key, top, end_ref, q_t, do_t, low_ref, ds_ref, dq_acc.at[j], d_acc.at[t],
                r_add,
            )

        def second_pass(t):
            def kept(h, part, cols):
                return e_ref[h, piece_rows(t, part), cols], g_ref[h, piece_rows(t, part), cols]

            add(
                t, block_rows(t), kept, lambda h: k_ref[h, block_rows(t), :],
                lambda h: top_ref[h, t, 0:1, :],
            )

        loop(j, REACH, lambda t: active(j, t), second_pass)
        if j == 0:
            for copy in kept_copies:
                copy.wait()
        for n, (query, t) in enumerate(LOCAL):
            if query == j:
                add(
                    t, slice(t * rows, (t + 1) * rows),
                    lambda h, part, cols: (
                        local_e[n * heads + h, part, cols], local_g[n * heads + h, part, cols]
                    ),
                    lambda h: local_k[(t - REACH) * heads + h],
                    lambda h: local_top[n * heads + h, 0:1, :],
                )

    def project(t):
        part = block_rows(t)
        grads = d_acc[t].astype(jnp.bfloat16)
        x_acc[:LATENT, part] += dot(w_ref[...], grads)
        gw_acc[...] += dot(lat_t_ref[:LATENT, part], grads, NT)

    loop(0, blocks, lambda t: (t >= REACH) | active(0, t) | active(1, t), project)
    dq0_ref[...] = (dq_acc[core] * SCALE).T.astype(dq0_ref.dtype)
    dq1_ref[...] = (dq_acc[1 - core] * SCALE).T.astype(dq1_ref.dtype)

    share = 2 * (LATENT // ranks)
    own_x = lax.rem(index_ref[0] // 2, 2)
    for i in range(ranks // 4):
        for out, x in ((keep_ref, own_x), (send_ref, 1 - own_x)):
            source = pl.multiple_of((2 * i + x) * share, share)
            out[i * share : (i + 1) * share, :] = gw_acc[pl.ds(source, share), :].astype(out.dtype)

    @pl.when(step == pl.num_programs(0) - 1)
    def _():
        places = ((x_old, 0), (x_far, 1 + core), (x_swap, 2 - core), (x_own, REACH + core),
                  (x_other, REACH + 1 - core))
        copies = []
        for i, (out, t) in enumerate(places):
            part = block_rows(t)
            lat_t_ref[:, part] = x_acc[:, part].astype(lat_t_ref.dtype)
            copies.append(pltpu.make_async_copy(lat_t_ref.at[:, part], out, sems.at[i]))
            copies[-1].start()
        for copy in copies:
            copy.wait()


def step_cols(height, size):
    return pl.BlockSpec((height, size), lambda i, index: (0, i))


def core_cols(height, size, first):
    def place(i, index):
        return (0, first(i, lax.rem(index[0], 2)))

    return pl.BlockSpec((height, size), place)


def step_block(*shape):
    return pl.BlockSpec((1, *shape), lambda i, index: (i, 0, 0, 0))


def fixed(*shape):
    return pl.BlockSpec(shape, lambda i, index: (0,) * len(shape))


SCALARS = pl.BlockSpec(memory_space=pltpu.SMEM)
ANYWHERE = pl.BlockSpec(memory_space=pl.ANY)


def call(body, steps, flops, in_specs, outs, scratch, name):
    return pl.pallas_call(
        body,
        grid_spec=pltpu.PrefetchScalarGridSpec(
            num_scalar_prefetch=1,
            grid=(steps,),
            in_specs=in_specs,
            out_specs=[spec for spec, _, _ in outs],
            scratch_shapes=[
                pltpu.VMEM(*entry) if isinstance(entry, tuple) else entry for entry in scratch
            ],
        ),
        out_shape=[jax.ShapeDtypeStruct(shape, kind) for _, shape, kind in outs],
        compiler_params=pltpu.CompilerParams(
            dimension_semantics=("arbitrary",), vmem_limit_bytes=58 * 1024 * 1024
        ),
        cost_estimate=pl.CostEstimate(
            flops=flops, bytes_accessed=16 * 1024 * 1024, transcendentals=0
        ),
        name=name,
    )


def head_specs(rows, heads, steps, first, in_place):
    def received(i, core):
        return first + i

    def own(i, core):
        return (core * steps if in_place else 0) + first + i

    return [
        core_cols(rows, heads * QK, own), core_cols(rows, heads * VDIM, own),
        core_cols(rows, heads * QK, received), core_cols(rows, heads * VDIM, received),
        core_cols(LATENT, heads * KV, own),
    ]


def local_scores(index, docs, inputs, latents, heads, steps, step, in_place):
    rows = inputs[0].shape[0]
    low, full = jnp.bfloat16, jnp.float32
    count = len(LOCAL) * heads
    return call(
        local_kernel,
        1,
        2 * heads * rows * rows * (3 * (QK + VDIM) + 2 * KV),
        [
            fixed(1, docs.shape[1]), *head_specs(rows, heads, steps, step, in_place),
            fixed(WIDTH, rows), fixed(WIDTH, rows),
        ],
        [
            (step_block(count, rows, rows), (1, count, rows, rows), low),
            (step_block(count, rows, rows), (1, count, rows, rows), low),
            (step_block(2 * heads, rows, QK), (1, 2 * heads, rows, QK), low),
            (step_block(2 * heads, 8, rows), (1, 2 * heads, 8, rows), full),
            (step_block(count, 8, rows), (1, count, 8, rows), full),
            (fixed(2, 8, rows), (2, 8, rows), jnp.int32),
        ],
        [
            ((2, rows, heads * QK), low),
            ((2, rows, heads * VDIM), low),
            ((2, rows, WIDTH), low),
            ((2 * heads, rows, VDIM), low),
            ((heads, rows, rows), full),
            ((heads, rows, rows), full),
        ],
        "local_scores",
    )(index, docs, *inputs, *latents)


def attention(index, doc_ids, inputs, kept, starts, latents, heads, steps, ranks, in_place):
    rows = inputs[0].shape[0]
    low, full = jnp.bfloat16, jnp.float32
    count = len(LOCAL) * heads
    window = (REACH + 2) * rows
    far = REACH * rows
    half = (LATENT // 2, steps * heads * KV)
    every = [entry for part in kept for entry in part]
    return call(
        functools.partial(main_kernel, ranks, steps),
        steps,
        2 * steps * heads * rows * rows * (5 * (QK + VDIM) + 8 * (2 * QK + VDIM) + 13 * KV),
        [SCALARS, *head_specs(rows, heads, steps, 0, in_place)]
        + [
            ANYWHERE, ANYWHERE, fixed(1, 2 * heads, rows, QK), fixed(1, 2 * heads, 8, rows),
            fixed(1, count, 8, rows),
        ]
        * steps
        + [fixed(2, 8, rows)]
        + [ANYWHERE] * len(latents),
        [(step_cols(rows, heads * QK), (rows, steps * heads * QK), low)] * 2
        + [(step_cols(LATENT // 2, heads * KV), half, low)] * 2
        + [(ANYWHERE, (WIDTH, rows), low)] * (REACH + 2),
        [
            ((2, rows, heads * QK), low),
            ((2, rows, heads * VDIM), low),
            ((far, WIDTH), low),
            ((WIDTH, window), low),
            ((heads, far, rows), low),
            ((heads, far, rows), low),
            ((heads, far, QK), low),
            ((heads, far, VDIM), low),
            ((heads, REACH, 8, rows), full),
            ((heads, 8, rows), full),
            ((heads, 8, rows), full),
            ((heads, rows, rows), full),
            ((heads, rows, rows), full),
            ((heads, rows, rows), low),
            ((heads, rows, rows), low),
            ((2, heads * QK, rows), full),
            ((REACH + 2, heads * KV, rows), full),
            ((LATENT, heads * KV), full),
            ((WIDTH, window), full),
            ((count, rows, rows), low),
            ((count, rows, rows), low),
            ((2 * heads, rows, QK), low),
            ((2 * heads, 8, rows), full),
            ((count, 8, rows), full),
            pltpu.SemaphoreType.DMA((5,)),
            pltpu.SemaphoreType.DMA((2,)),
        ],
        "attention",
    )(index, doc_ids, *inputs, *every, starts, *latents)


def permute(value, axis, target):
    count = lax.axis_size(axis)
    pairs = [(s, target(s)) for s in range(count) if 0 <= target(s) < count]
    return lax.ppermute(value, axis, pairs)


def local(kv_latent, queries, grad_out, kv_up_weight, doc_ids):
    ranks = lax.axis_size("ctx")
    position = lax.axis_index("ctx").astype(jnp.int32)
    index, core = position[None], lax.rem(position, 2)
    low, full = jnp.bfloat16, jnp.float32
    docs = doc_ids[None]
    core_heads = kv_up_weight.shape[1] // KV // 2
    heads = min(2, core_heads)
    steps = core_heads // heads

    def own_heads(value, which):
        size = value.shape[1] // 2
        return lax.dynamic_slice_in_dim(value, which * size, size, axis=1)

    def across(value):
        return permute(value, "ctx", lambda s: s ^ 1)

    latent = kv_latent.T
    far = permute(latent, "ctx", lambda s: s + 2)
    mixed = permute(latent, "ctx", lambda s: s + 3 if s % 2 else -1)
    other = across(latent)
    in_place = heads * QK % 128 == 0
    inputs = (
        queries if in_place else own_heads(queries, core),
        grad_out if in_place else own_heads(grad_out, core),
        across(own_heads(queries, 1 - core)),
        across(own_heads(grad_out, 1 - core)),
        kv_up_weight if in_place else own_heads(kv_up_weight, core),
    )
    kept = []
    for step in range(steps):
        *parts, starts = local_scores(
            index, docs, inputs, (latent, other), heads, steps, step, in_place
        )
        kept.append(parts)
        if step == 0:
            far, mixed, parts[-1] = lax.optimization_barrier((far, mixed, parts[-1]))
            swapped = across(far)
            passed = permute(mixed, "ctx", lambda s: -1 if s % 2 else s + 1)

    dq_own, dq_other, keep, send, to_old, to_far, to_swap, mine, to_other = attention(
        index, doc_ids, inputs, kept, starts,
        (far, swapped, mixed, passed, latent, other), heads, steps, ranks, in_place,
    )

    from_x = permute(send, "ctx", lambda s: s ^ 2)
    from_swap = across(to_swap)
    from_other = across(to_other)
    from_old = permute(to_old, "ctx", lambda s: s - 1 if s % 2 else -1)
    far_sum = (to_far.astype(full) + from_swap.astype(full)).astype(low)
    old_sum = (to_old.astype(full) + from_old.astype(full)).astype(low)
    from_x, *_ = lax.optimization_barrier((from_x, far_sum, old_sum))
    from_far = permute(far_sum, "ctx", lambda s: s - 2)
    from_mixed = permute(old_sum, "ctx", lambda s: -1 if s % 2 else s - 3)
    plane = (keep.astype(full) + from_x.astype(full)).astype(low)
    columns = [list(range(first, ranks, 4)) for first in range(4)]
    pieces = lax.all_to_all(plane, "ctx", 0, 0, axis_index_groups=columns, tiled=True)
    share = LATENT // ranks
    summed = jnp.sum(pieces.reshape(ranks // 4, 2 * share, -1).astype(full), axis=0)

    def in_order(own, received):
        first = jnp.where(core == 0, own, received)
        second = jnp.where(core == 0, received, own)
        return jnp.concatenate([first, second], axis=1)

    rows_own = lax.dynamic_slice_in_dim(summed, core * share, share, axis=0)
    rows_other = lax.dynamic_slice_in_dim(summed, (1 - core) * share, share, axis=0)
    grad_weight = in_order(rows_own, across(rows_other))
    grad_queries = in_order(dq_own, across(dq_other))

    total = mine.astype(full) + from_other.astype(full)
    total = total + from_mixed.astype(full) + from_far.astype(full)
    mine = total.astype(low)
    size = lax.axis_size("head")
    for turn in range(1, size):
        other = lax.ppermute(mine, "head", [(s, (s + turn) % size) for s in range(size)])
        total = total + other.astype(full)
    return grad_queries, total.astype(low).T, grad_weight


def solution(mesh):
    return jax.shard_map(
        local,
        mesh=mesh,
        in_specs=(P("ctx", None), P("ctx", "head"), P("ctx", "head"), P(None, "head"), P()),
        out_specs=(P("ctx", "head"), P("ctx", None), P("ctx", "head")),
        check_vma=False,
    )
```

profile of v0, /device:TPU:10, one launch (start us, length us, event | category | flops | bytes accessed | tf_op | source)
XLA Modules:
  0.0 140.4 jit_solution(157927776403826630)
XLA Ops:
  0.6 0.0 copy-start
  0.6 0.0 copy-start.2
  0.7 2.2 %constant_dynamic-slice_fusion.2 = bf16[512,768]{1,0:T(8,128)(2,1)} fusion(bf16[512,1536]{1,0:T(8,128)(2,1)} %q0.5, s32[]{:T(128)S(6)} %select_n.37), kind=kLoop, calls=%fused_computation.16 | loop fusion | bytes 1572868 | tf_op jit(solution)/shard_map/dynamic_slice | solution.py:561
  2.8 0.0 collective-permute-start
  2.9 0.5 collective-permute-start.2
  3.4 0.1 collective-permute-start.1
  3.5 3.5 %collective-permute-start.3 = (bf16[576,512]{1,0:T(8,128)(2,1)S(1)}, bf16[576,512]{1,0:T(8,128)(2,1)S(1)}, u32[]{:S(2)}, u32[]{:S(2)}) collective-permute-start(bf16[576,512]{1,0:T(8,128)(2,1)S(1)} %bitcast.10), channel_id=1, source_target_pairs={{0,4},{2,6},{4,8},{6,10},{8,12},{10,14},{12,16},{14,18},{16,20},{1... | collective-permute-start | bytes 1769480 | tf_op jit(solution)/shard_map/ppermute | solution.py:546
  7.0 1.3 collective-permute-start.4
  8.3 0.0 collective-permute-done.2.lat1.refs_16_
  8.3 0.0 copy-start.3
  8.3 0.7 copy-done.5
  9.0 0.2 copy-done.3
  9.3 0.3 copy-done.1
  9.5 9.0 %local_scores.2 = (bf16[1,6,512,512]{3,2,1,0:T(8,128)(2,1)}, bf16[1,6,512,512]{3,2,1,0:T(8,128)(2,1)}, bf16[1,4,512,192]{3,2,1,0:T(8,128)(2,1)}, f32[1,4,8,512]{...) custom-call(s32[1]{0:T(128)} %bitcast.index_ref, s32[1,8192]{1,0:T(1,128)} %bitcast.12, ...), custom_call_target="tpu_custom_call" | custom-call | flops 1543503872 | bytes 16777216 | tf_op jit(solution)/shard_map/local_scores/pallas_call | solution.py:460
  18.5 2.6 %collective-permute-done.3.refs_11_ = bf16[576,512]{1,0:T(8,128)(2,1)S(1)} collective-permute-done((bf16[576,512]{1,0:T(8,128)(2,1)S(1)}, bf16[576,512]{1,0:T(8,128)(2,1)S(1)}, u32[]{:S(2)}, u32[]{:S(2)}) %collective-permute-start.3) | collective-permute-done | bytes 589856 | tf_op jit(solution)/shard_map/ppermute | solution.py:546
  21.1 6.3 %collective-permute-done.4.refs_13_ = bf16[576,512]{1,0:T(8,128)(2,1)S(1)} collective-permute-done((bf16[576,512]{1,0:T(8,128)(2,1)S(1)}, bf16[576,512]{1,0:T(8,128)(2,1)S(1)}, u32[]{:S(2)}, u32[]{:S(2)}) %collective-permute-start.4) | collective-permute-done | bytes 589856 | tf_op jit(solution)/shard_map/ppermute | solution.py:546
  27.4 2.4 %collective-permute-start.6 = (bf16[576,512]{1,0:T(8,128)(2,1)S(1)}, bf16[576,512]{1,0:T(8,128)(2,1)S(1)}, u32[]{:S(2)}, u32[]{:S(2)}) collective-permute-start(bf16[576,512]{1,0:T(8,128)(2,1)S(1)} %collective-permute-done.4.refs_13_), channel_id=1, source_target_pairs={{0,2},{4,6},{8,10},{12,14},{16,18},{20,22},{24,26},{28,30},{1,3},{... | collective-permute-start | bytes 1769480 | tf_op jit(solution)/shard_map/ppermute | solution.py:546
  29.8 9.0 %local_scores.3 = (bf16[1,6,512,512]{3,2,1,0:T(8,128)(2,1)}, bf16[1,6,512,512]{3,2,1,0:T(8,128)(2,1)}, bf16[1,4,512,192]{3,2,1,0:T(8,128)(2,1)}, f32[1,4,8,512]{...) custom-call(s32[1]{0:T(128)} %bitcast.index_ref, s32[1,8192]{1,0:T(1,128)} %bitcast.13, ...), custom_call_target="tpu_custom_call" | custom-call | flops 1543503872 | bytes 16777216 | tf_op jit(solution)/shard_map/local_scores/pallas_call | solution.py:460
  38.8 0.0 collective-permute-done.5.refs_12_
  38.9 0.8 copy-done.11
  39.7 0.2 copy-done.12
  39.9 37.1 %attention.1 = (bf16[512,768]{1,0:T(8,128)(2,1)}, bf16[512,768]{1,0:T(8,128)(2,1)}, bf16[256,1024]{1,0:T(8,128)(2,1)}, bf16[256,1024]{1,0:T(8,128)(2,1)}, bf16[5...) custom-call(s32[1]{0:T(128)} %bitcast.index_ref, ...), custom_call_target="tpu_custom_call" | custom-call | flops 18924699648 | bytes 16777216 | tf_op jit(solution)/shard_map/attention/pallas_call | solution.py:496
  77.0 1.4 %collective-permute-start.9 = (bf16[576,512]{1,0:T(8,128)(2,1)}, bf16[576,512]{1,0:T(8,128)(2,1)S(1)}, u32[]{:S(2)}, u32[]{:S(2)}) collective-permute-start(bf16[576,512]{1,0:T(8,128)(2,1)} %get-tuple-element.45), channel_id=1, source_target_pairs={{2,0},{6,4},{10,8},{14,12},{18,16},{22,20},{26,24},{30,28},{3,1},{... | collective-permute-start | bytes 1769480 | tf_op jit(solution)/shard_map/ppermute | solution.py:546
  78.4 1.2 collective-permute-start.11
  79.7 8.7 %collective-permute-start.14 = (bf16[256,1024]{1,0:T(8,128)(2,1)}, bf16[256,1024]{1,0:T(8,128)(2,1)S(1)}, u32[]{:S(2)}, u32[]{:S(2)}) collective-permute-start(bf16[256,1024]{1,0:T(8,128)(2,1)} %get-tuple-element.49), channel_id=1, source_target_pairs={{0,4},{2,6},{4,0},{6,2},{8,12},{10,14},{12,8},{14,10},{16,20},{18,... | collective-permute-start | bytes 1572872 | tf_op jit(solution)/shard_map/ppermute | solution.py:546
  88.3 0.0 collective-permute-start.8
  88.3 0.5 collective-permute-start.7
  88.9 2.0 %add_convert_fusion.2 = bf16[576,512]{1,0:T(8,128)(2,1)} fusion(bf16[576,512]{1,0:T(8,128)(2,1)S(1)} %collective-permute-done.9, bf16[576,512]{1,0:T(8,128)(2,1)} %get-tuple-element.45), kind=kLoop, calls=%fused_computation.4 | loop fusion | flops 1179648 | bytes 1769472 | tf_op jit(solution)/shard_map/convert_element_type | solution.py:599
  90.9 1.4 %collective-permute-start.10 = (bf16[576,512]{1,0:T(8,128)(2,1)}, bf16[576,512]{1,0:T(8,128)(2,1)S(1)}, u32[]{:S(2)}, u32[]{:S(2)}) collective-permute-start(bf16[576,512]{1,0:T(8,128)(2,1)} %add_convert_fusion.2), channel_id=1, source_target_pairs={{8,2},{12,6},{16,10},{20,14},{24,18},{28,22},{9,3},{13,7},{17,11},... | collective-permute-start | bytes 1769480 | tf_op jit(solution)/shard_map/ppermute | solution.py:546
  92.4 1.0 add_convert_fusion.1
  93.3 3.0 %collective-permute-start.12 = (bf16[576,512]{1,0:T(8,128)(2,1)}, bf16[576,512]{1,0:T(8,128)(2,1)}, u32[]{:S(2)}, u32[]{:S(2)}) collective-permute-start(bf16[576,512]{1,0:T(8,128)(2,1)} %add_convert_fusion.1), channel_id=1, source_target_pairs={{4,0},{6,2},{8,4},{10,6},{12,8},{14,10},{16,12},{18,14},{20,16},{2... | collective-permute-start | bytes 1769480 | tf_op jit(solution)/shard_map/ppermute | solution.py:546
  96.3 4.6 %collective-permute-done.14 = bf16[256,1024]{1,0:T(8,128)(2,1)S(1)} collective-permute-done((bf16[256,1024]{1,0:T(8,128)(2,1)}, bf16[256,1024]{1,0:T(8,128)(2,1)S(1)}, u32[]{:S(2)}, u32[]{:S(2)}) %collective-permute-start.14) | collective-permute-done | bytes 524320 | tf_op jit(solution)/shard_map/ppermute | solution.py:546
  101.0 1.0 add_convert_fusion.3
  101.9 12.5 %all-to-all-start = ((bf16[4,64,1024]{2,1,0:T(8,128)(2,1)}), bf16[4,64,1024]{2,1,0:T(8,128)(2,1)}, u32[]{:S(2)}, u32[]{:S(2)}) async-start(bf16[4,64,1024]{2,1,0:T(8,128)(2,1)} %bitcast.4), calls=%async_computation | async-start | bytes 1048576 | tf_op jit(solution)/shard_map/all_to_all | solution.py:605
  114.4 0.0 collective-permute-done.7
  114.4 0.9 copy-done.6
  115.3 1.5 %broadcast_select_fusion.1 = (bf16[512,768]{1,0:T(8,128)(2,1)S(1)}, bf16[512,768]{1,0:T(8,128)(2,1)S(1)}) fusion(bf16[512,768]{1,0:T(8,128)(2,1)} %get-tuple-element.41, bf16[512,768]{1,0:T(8,128)(2,1)} %copy-done.6, pred[]{:T(512)S(6)} %eq.2), kind=kLoop, calls=%fused_computation.8 | loop fusion | flops 786432 | bytes 3145729 | tf_op jit(solution)/shard_map/jit(_where)/select_n | solution.py:610
  116.9 0.0 collective-permute-done.8
  116.9 8.7 %collective-permute-done.12 = bf16[576,512]{1,0:T(8,128)(2,1)} collective-permute-done((bf16[576,512]{1,0:T(8,128)(2,1)}, bf16[576,512]{1,0:T(8,128)(2,1)}, u32[]{:S(2)}, u32[]{:S(2)}) %collective-permute-start.12) | collective-permute-done | bytes 589856 | tf_op jit(solution)/shard_map/ppermute | solution.py:546
  125.6 2.2 %fusion.1 = bf16[576,512]{1,0:T(8,128)(2,1)} fusion(bf16[576,512]{1,0:T(8,128)(2,1)} %collective-permute-done.12, bf16[576,512]{1,0:T(8,128)(2,1)S(1)} %collective-permute-done.10, bf16[576,512]{1,0:T(8,128)(2,1)S(1)} %collective-permute-done.8, bf16[576,512]{1,0:T(8,128)(2,1)S(1)} %copy-done.4), kind=kLoop, calls=%fused_computation.10 | loop fusion | flops 2359296 | bytes 2949120 | tf_op jit(solution)/shard_map/convert_element_type | solution.py:621
  127.7 1.5 %collective-permute-start.13 = (bf16[576,512]{1,0:T(8,128)(2,1)}, bf16[576,512]{1,0:T(8,128)(2,1)}, u32[]{:S(2)}, u32[]{:S(2)}) collective-permute-start(bf16[576,512]{1,0:T(8,128)(2,1)} %fusion.1), channel_id=1, source_target_pairs={{0,1},{1,0},{2,3},{3,2},{4,5},{5,4},{6,7},{7,6},{8,9},{9,8},{10,11... | collective-permute-start | bytes 1769480 | tf_op jit(solution)/shard_map/ppermute | solution.py:624
  129.3 1.1 convert_reduce_fusion
  130.4 0.1 collective-permute-start.15
  130.5 1.3 pad_maximum_fusion
  131.8 0.1 collective-permute-done.15
  131.9 0.7 pad_maximum_fusion.1
  132.6 5.3 %collective-permute-done.13 = bf16[576,512]{1,0:T(8,128)(2,1)} collective-permute-done((bf16[576,512]{1,0:T(8,128)(2,1)}, bf16[576,512]{1,0:T(8,128)(2,1)}, u32[]{:S(2)}, u32[]{:S(2)}) %collective-permute-start.13) | collective-permute-done | bytes 589856 | tf_op jit(solution)/shard_map/ppermute | solution.py:624
  137.9 2.4 %fusion = bf16[512,576]{0,1:T(8,128)(2,1)} fusion(bf16[576,512]{1,0:T(8,128)(2,1)} %collective-permute-done.13, bf16[576,512]{1,0:T(8,128)(2,1)} %collective-permute-done.12, bf16[576,512]{1,0:T(8,128)(2,1)S(1)} %collective-permute-done.10, bf16[576,512]{1,0:T(8,128)(2,1)S(1)} %collective-permute-done.8, bf16[576,512]{1,0:T(8,128)(2,1)S(1)} %copy-done.4), kind=kLoop, calls=%fused_computation.9 | loop fusion | flops 2949120 | bytes 3538944 | tf_op jit(solution)/shard_map/transpose | solution.py:626
  (28 shorter events, 0.1 us)
Async XLA Ops:
  0.6 2.7 %copy-start = (bf16[512,1024]{1,0:T(8,128)(2,1)S(1)}, bf16[512,1024]{1,0:T(8,128)(2,1)}, u32[]{:S(2)}) copy-start(bf16[512,1024]{1,0:T(8,128)(2,1)} %do0.5) | copy-start | bytes 3145732
  0.6 2.8 %copy-start.2 = (bf16[512,576]{0,1:T(8,128)(2,1)S(1)}, bf16[512,576]{0,1:T(8,128)(2,1)}, u32[]{:S(2)}) copy-start(bf16[512,576]{0,1:T(8,128)(2,1)} %param.5) | copy-start | bytes 1769476
  2.8 5.5 %collective-permute-start = (bf16[512,768]{1,0:T(8,128)(2,1)}, bf16[512,768]{1,0:T(8,128)(2,1)S(1)}, u32[]{:S(2)}, u32[]{:S(2)}) collective-permute-start(bf16[512,768]{1,0:T(8,128)(2,1)} %constant_dynamic-slice_fusion.2), channel_id=1, source_target_pairs={{0,2},{2,0},{4,6},{6,4},{8,10},{10,8},{12,14},{14,12},{16,18},{18,... | collective-permute-start | bytes 2359304 | tf_op jit(solution)/shard_map/ppermute | solution.py:546
  2.9 5.4 %collective-permute-start.2 = (bf16[576,512]{1,0:T(8,128)(2,1)}, bf16[576,512]{1,0:T(8,128)(2,1)S(1)}, u32[]{:S(2)}, u32[]{:S(2)}) collective-permute-start(bf16[576,512]{1,0:T(8,128)(2,1)} %bitcast.6), channel_id=1, source_target_pairs={{0,2},{2,0},{4,6},{6,4},{8,10},{10,8},{12,14},{14,12},{16,18},{18,... | collective-permute-start | bytes 1769480 | tf_op jit(solution)/shard_map/ppermute | solution.py:546
  3.4 4.9 %collective-permute-start.1 = (bf16[512,512]{1,0:T(8,128)(2,1)S(1)}, bf16[512,512]{1,0:T(8,128)(2,1)S(1)}, u32[]{:S(2)}, u32[]{:S(2)}) collective-permute-start(bf16[512,512]{1,0:T(8,128)(2,1)S(1)} %constant_dynamic-slice_fusion.1), channel_id=1, source_target_pairs={{0,2},{2,0},{4,6},{6,4},{8,10},{10,8},{12,14},{14,12},{16,18},{18,... | collective-permute-start | bytes 1572872 | tf_op jit(solution)/shard_map/ppermute | solution.py:546
  3.5 17.6 %collective-permute-start.3 = (bf16[576,512]{1,0:T(8,128)(2,1)S(1)}, bf16[576,512]{1,0:T(8,128)(2,1)S(1)}, u32[]{:S(2)}, u32[]{:S(2)}) collective-permute-start(bf16[576,512]{1,0:T(8,128)(2,1)S(1)} %bitcast.10), channel_id=1, source_target_pairs={{0,4},{2,6},{4,8},{6,10},{8,12},{10,14},{12,16},{14,18},{16,20},{1... | collective-permute-start | bytes 1769480 | tf_op jit(solution)/shard_map/ppermute | solution.py:546
  7.0 20.4 %collective-permute-start.4 = (bf16[576,512]{1,0:T(8,128)(2,1)S(1)}, bf16[576,512]{1,0:T(8,128)(2,1)S(1)}, u32[]{:S(2)}, u32[]{:S(2)}) collective-permute-start(bf16[576,512]{1,0:T(8,128)(2,1)S(1)} %bitcast.11), channel_id=1, source_target_pairs={{2,8},{6,12},{10,16},{14,20},{18,24},{22,28},{3,9},{7,13},{11,17},... | collective-permute-start | bytes 1769480 | tf_op jit(solution)/shard_map/ppermute | solution.py:546
  8.3 0.8 copy-start.5
  8.3 1.0 copy-start.3
  8.3 1.2 copy-start.1
  21.1 17.7 %copy-start.9 = (bf16[576,512]{1,0:T(8,128)(2,1)}, bf16[576,512]{1,0:T(8,128)(2,1)S(1)}, u32[]{:S(2)}) copy-start(bf16[576,512]{1,0:T(8,128)(2,1)S(1)} %collective-permute-done.3.refs_11_) | copy-start | bytes 1769476
  27.4 11.4 %copy-start.10 = (bf16[576,512]{1,0:T(8,128)(2,1)}, bf16[576,512]{1,0:T(8,128)(2,1)S(1)}, u32[]{:S(2)}) copy-start(bf16[576,512]{1,0:T(8,128)(2,1)S(1)} %collective-permute-done.4.refs_13_) | copy-start | bytes 1769476
  27.4 11.5 %collective-permute-start.5 = (bf16[576,512]{1,0:T(8,128)(2,1)S(1)}, bf16[576,512]{1,0:T(8,128)(2,1)S(1)}, u32[]{:S(2)}, u32[]{:S(2)}) collective-permute-start(bf16[576,512]{1,0:T(8,128)(2,1)S(1)} %collective-permute-done.3.refs_11_), channel_id=1, source_target_pairs={{0,2},{2,0},{4,6},{6,4},{8,10},{10,8},{12,14},{14,12},{16,18},{18,... | collective-permute-start | bytes 1769480 | tf_op jit(solution)/shard_map/ppermute | solution.py:546
  27.4 11.5 %collective-permute-start.6 = (bf16[576,512]{1,0:T(8,128)(2,1)S(1)}, bf16[576,512]{1,0:T(8,128)(2,1)S(1)}, u32[]{:S(2)}, u32[]{:S(2)}) collective-permute-start(bf16[576,512]{1,0:T(8,128)(2,1)S(1)} %collective-permute-done.4.refs_13_), channel_id=1, source_target_pairs={{0,2},{4,6},{8,10},{12,14},{16,18},{20,22},{24,26},{28,30},{1,3},{... | collective-permute-start | bytes 1769480 | tf_op jit(solution)/shard_map/ppermute | solution.py:546
  38.8 0.8 copy-start.11
  38.9 1.0 copy-start.12
  77.0 15.4 %copy-start.7 = (bf16[576,512]{1,0:T(8,128)(2,1)S(1)}, bf16[576,512]{1,0:T(8,128)(2,1)}, u32[]{:S(2)}) copy-start(bf16[576,512]{1,0:T(8,128)(2,1)} %get-tuple-element.46) | copy-start | bytes 1769476
  77.0 11.8 %collective-permute-start.9 = (bf16[576,512]{1,0:T(8,128)(2,1)}, bf16[576,512]{1,0:T(8,128)(2,1)S(1)}, u32[]{:S(2)}, u32[]{:S(2)}) collective-permute-start(bf16[576,512]{1,0:T(8,128)(2,1)} %get-tuple-element.45), channel_id=1, source_target_pairs={{2,0},{6,4},{10,8},{14,12},{18,16},{22,20},{26,24},{30,28},{3,1},{... | collective-permute-start | bytes 1769480 | tf_op jit(solution)/shard_map/ppermute | solution.py:546
  78.4 13.9 %collective-permute-start.11 = (bf16[576,512]{1,0:T(8,128)(2,1)}, bf16[576,512]{1,0:T(8,128)(2,1)S(1)}, u32[]{:S(2)}, u32[]{:S(2)}) collective-permute-start(bf16[576,512]{1,0:T(8,128)(2,1)} %get-tuple-element.47), channel_id=1, source_target_pairs={{0,2},{2,0},{4,6},{6,4},{8,10},{10,8},{12,14},{14,12},{16,18},{18,... | collective-permute-start | bytes 1769480 | tf_op jit(solution)/shard_map/ppermute | solution.py:546
  79.7 21.3 %collective-permute-start.14 = (bf16[256,1024]{1,0:T(8,128)(2,1)}, bf16[256,1024]{1,0:T(8,128)(2,1)S(1)}, u32[]{:S(2)}, u32[]{:S(2)}) collective-permute-start(bf16[256,1024]{1,0:T(8,128)(2,1)} %get-tuple-element.49), channel_id=1, source_target_pairs={{0,4},{2,6},{4,0},{6,2},{8,12},{10,14},{12,8},{14,10},{16,20},{18,... | collective-permute-start | bytes 1572872 | tf_op jit(solution)/shard_map/ppermute | solution.py:546
  88.3 28.5 %collective-permute-start.8 = (bf16[576,512]{1,0:T(8,128)(2,1)}, bf16[576,512]{1,0:T(8,128)(2,1)S(1)}, u32[]{:S(2)}, u32[]{:S(2)}) collective-permute-start(bf16[576,512]{1,0:T(8,128)(2,1)} %get-tuple-element.44), channel_id=1, source_target_pairs={{0,2},{2,0},{4,6},{6,4},{8,10},{10,8},{12,14},{14,12},{16,18},{18,... | collective-permute-start | bytes 1769480 | tf_op jit(solution)/shard_map/ppermute | solution.py:546
  88.3 26.1 %collective-permute-start.7 = (bf16[512,768]{1,0:T(8,128)(2,1)}, bf16[512,768]{1,0:T(8,128)(2,1)S(1)}, u32[]{:S(2)}, u32[]{:S(2)}) collective-permute-start(bf16[512,768]{1,0:T(8,128)(2,1)} %get-tuple-element.42), channel_id=1, source_target_pairs={{0,2},{2,0},{4,6},{6,4},{8,10},{10,8},{12,14},{14,12},{16,18},{18,... | collective-permute-start | bytes 2359304 | tf_op jit(solution)/shard_map/ppermute | solution.py:546
  90.9 10.1 %copy-start.8 = (bf16[256,1024]{1,0:T(8,128)(2,1)S(1)}, bf16[256,1024]{1,0:T(8,128)(2,1)}, u32[]{:S(2)}) copy-start(bf16[256,1024]{1,0:T(8,128)(2,1)} %get-tuple-element.48) | copy-start | bytes 1572868
  90.9 26.0 %collective-permute-start.10 = (bf16[576,512]{1,0:T(8,128)(2,1)}, bf16[576,512]{1,0:T(8,128)(2,1)S(1)}, u32[]{:S(2)}, u32[]{:S(2)}) collective-permute-start(bf16[576,512]{1,0:T(8,128)(2,1)} %add_convert_fusion.2), channel_id=1, source_target_pairs={{8,2},{12,6},{16,10},{20,14},{24,18},{28,22},{9,3},{13,7},{17,11},... | collective-permute-start | bytes 1769480 | tf_op jit(solution)/shard_map/ppermute | solution.py:546
  93.3 32.2 %collective-permute-start.12 = (bf16[576,512]{1,0:T(8,128)(2,1)}, bf16[576,512]{1,0:T(8,128)(2,1)}, u32[]{:S(2)}, u32[]{:S(2)}) collective-permute-start(bf16[576,512]{1,0:T(8,128)(2,1)} %add_convert_fusion.1), channel_id=1, source_target_pairs={{4,0},{6,2},{8,4},{10,6},{12,8},{14,10},{16,12},{18,14},{20,16},{2... | collective-permute-start | bytes 1769480 | tf_op jit(solution)/shard_map/ppermute | solution.py:546
  101.9 27.3 %all-to-all-start = ((bf16[4,64,1024]{2,1,0:T(8,128)(2,1)}), bf16[4,64,1024]{2,1,0:T(8,128)(2,1)}, u32[]{:S(2)}, u32[]{:S(2)}) async-start(bf16[4,64,1024]{2,1,0:T(8,128)(2,1)} %bitcast.4), calls=%async_computation | async-start | bytes 1048576 | tf_op jit(solution)/shard_map/all_to_all | solution.py:605
  114.4 0.9 copy-start.6
  115.3 10.2 %copy-start.4 = (bf16[576,512]{1,0:T(8,128)(2,1)S(1)}, bf16[576,512]{1,0:T(8,128)(2,1)}, u32[]{:S(2)}) copy-start(bf16[576,512]{1,0:T(8,128)(2,1)} %get-tuple-element.43) | copy-start | bytes 1769476
  127.7 10.2 %collective-permute-start.13 = (bf16[576,512]{1,0:T(8,128)(2,1)}, bf16[576,512]{1,0:T(8,128)(2,1)}, u32[]{:S(2)}, u32[]{:S(2)}) collective-permute-start(bf16[576,512]{1,0:T(8,128)(2,1)} %fusion.1), channel_id=1, source_target_pairs={{0,1},{1,0},{2,3},{3,2},{4,5},{5,4},{6,7},{7,6},{8,9},{9,8},{10,11... | collective-permute-start | bytes 1769480 | tf_op jit(solution)/shard_map/ppermute | solution.py:624
  130.4 1.4 %collective-permute-start.15 = (f32[32,1024]{1,0:T(8,128)S(1)}, f32[32,1024]{1,0:T(8,128)S(1)}, u32[]{:S(2)}, u32[]{:S(2)}) collective-permute-start(f32[32,1024]{1,0:T(8,128)S(1)} %constant_dynamic-slice_fusion), channel_id=1, source_target_pairs={{0,2},{2,0},{4,6},{6,4},{8,10},{10,8},{12,14},{14,12},{16,18},{18,... | collective-permute-start | bytes 393224 | tf_op jit(solution)/shard_map/ppermute | solution.py:546
where the time goes:
time: 143 us; the launch traced here: 140 us
  Pallas kernels  55.1 us (39%)
  starting transfers between devices  38.1 us (27%)
  waiting for transfers between devices  27.6 us (19%)
  other arithmetic  13.3 us (9%)
  local copies, waits for them, and re-layouts  5.37 us (4%)
    pallas_call x1, Pallas kernels, attention(): call(functools.partial(main_kernel, ranks, steps), steps, 2 * steps * hea...  37.1 us
    ppermute x15, starting transfers between devices, permute(): return lax.ppermute(value, axis, pairs)  24.1 us
    ppermute x15, waiting for transfers between devices, permute(): return lax.ppermute(value, axis, pairs)  22.3 us
    pallas_call x2, Pallas kernels, local_scores(): call(local_kernel, 1, 2 * heads * rows * rows * (3 * (QK + VDIM) + 2 * KV...  18 us
    all_to_all x1, starting transfers between devices, local(): lax.all_to_all(plane, 'ctx', 0, 0, axis_index_groups=columns, tiled=True)  12.5 us
    ppermute x1, waiting for transfers between devices, local(): lax.ppermute(mine, 'head', [(s, (s + turn) % size) for s in range(size)])  5.34 us
    unnamed x26, local copies, waits for them, and re-layouts  3.13 us
  transfers between devices with their start and end apart: 17, of which 6 were waited for; matrix products, arithmetic and copies ran while one was open for 8% of the time, Pallas kernels for 13%

commit v1 on v0

--- a/solution.py
+++ b/solution.py
@@ -63,20 +63,20 @@
         for c in range(0, rows, LANES):
             cols = slice(c, c + LANES)
 
-            def scores(part):
-                place = index + part.start
-                seen = (place >= lower[:, cols]) & (place <= upper[:, cols])
-                return jnp.where(seen, raw_ref[h, part, cols] * SCALE2, MASKED)
-
             high = None
             for part in pieces:
-                piece = fold(scores(part), jnp.max)
+                seen = index >= lower[:, cols] - part.start
+                if upper is not None:
+                    seen = seen & (index <= upper[:, cols] - part.start)
+                scores = jnp.where(seen, raw_ref[h, part, cols] * SCALE2, MASKED)
+                raw_ref[h, part, cols] = scores
+                piece = fold(scores, jnp.max)
                 high = piece if high is None else jnp.maximum(high, piece)
             old_top = run_ref[h, 0:1, cols]
             new_top = jnp.maximum(old_top, jnp.max(high, axis=0, keepdims=True))
             mass, cross = 0.0, 0.0
             for part in pieces:
-                weights = jnp.exp2(scores(part) - new_top)
+                weights = jnp.exp2(raw_ref[h, part, cols] - new_top)
                 grads = graw_ref[h, part, cols]
                 keep(h, part, cols, weights.astype(jnp.bfloat16), grads.astype(jnp.bfloat16))
                 mass = mass + fold(weights, jnp.sum)
@@ -91,7 +91,10 @@
             )
 
 
-def grad_block(kept, key, top, end_ref, q_t, do_t, low_ref, ds_ref, dq_acc, d_acc, r_add):
+def grad_block(kept, key, top, end_ref, q_t, do_t, low_ref, ds_ref, dq_acc, d_acc, r_acc, first_q, first_k):
+    def put(ref, part, value, first):
+        ref[part, :] = value if first else ref[part, :] + value
+
     rows = do_t.shape[1]
     heads = range(do_t.shape[0] // VDIM)
     for h in heads:
@@ -111,11 +114,11 @@
     for h in heads:
         dvalue = dot(do_t[head_cols(h, VDIM), :], low_ref[h], NT)
         dkey = dot(q_t[head_cols(h, QK), :], ds_ref[h], NT) * SCALE
-        dq_acc[head_cols(h, QK), :] += dot(key(h).T, ds_ref[h])
-        d_acc[h * KV : h * KV + NOPE, :] += dkey[:NOPE]
-        d_acc[h * KV + NOPE : (h + 1) * KV, :] += dvalue
+        put(dq_acc, head_cols(h, QK), dot(key(h).T, ds_ref[h]), first_q)
+        put(d_acc, slice(h * KV, h * KV + NOPE), dkey[:NOPE], first_k)
+        put(d_acc, slice(h * KV + NOPE, (h + 1) * KV), dvalue, first_k)
         rope = rope + dkey[NOPE:]
-    r_add(rope)
+    put(r_acc, slice(0, ROPE), rope, first_k)
 
 
 def start_stats(run_ref):
@@ -140,8 +143,8 @@
 
 def query_bounds(start_ref, chip, j, t, rows):
     lower = start_ref[j, 0:1, :] - (chip + t - REACH) * rows
-    upper = lax.broadcasted_iota(jnp.int32, (1, rows), 1) + (j + REACH - t) * rows
-    return lower, upper
+    own = isinstance(t, int) and t == j + REACH
+    return lower, lax.broadcasted_iota(jnp.int32, (1, rows), 1) if own else None
 
 
 def find_starts(docs_ref, start_ref, chip, rows):
@@ -206,40 +209,26 @@
             top_ref[0, n * heads + h] = run[h]
 
 
-def main_kernel(ranks, steps, index_ref, docs_sref, q0, do0, q1, do1, w_ref, *refs):
-    kept, refs = [refs[5 * n : 5 * n + 5] for n in range(steps)], refs[5 * steps :]
-    main_body(ranks, index_ref, docs_sref, q0, do0, q1, do1, w_ref, kept, *refs)
-
-
-def main_body(
-    ranks, index_ref, docs_sref, q0, do0, q1, do1, w_ref, kept_steps, start_ref,
+def main_kernel(
+    ranks,
+    index_ref, docs_sref, q0, do0, q1, do1, w_ref,
+    all_e, all_g, local_k, local_run, local_top, start_ref,
     lat_far, lat_swap, lat_mixed, lat_passed, lat_own, lat_other,
     dq0_ref, dq1_ref, keep_ref, send_ref, x_old, x_far, x_swap, x_own, x_other,
     q_ref, do_ref, lat_ref, lat_t_ref, e_ref, g_ref, k_ref, v_ref, top_ref,
     run_ref, end_ref, raw_ref, graw_ref, low_ref, ds_ref, dq_acc, d_acc, gw_acc, x_acc,
-    local_e, local_g, local_k, local_run, local_top, sems, kept_sems,
+    r_acc, local_e, local_g, sems, kept_sems,
 ):
     step = pl.program_id(0)
     rows = q0.shape[0]
     heads = w_ref.shape[1] // KV
     blocks = REACH + 2
-
-    kept_copies = []
-    for n, (all_e, all_g, all_k, all_run, all_top) in enumerate(kept_steps):
-        copies = [
-            pltpu.make_async_copy(all_e.at[0], local_e, kept_sems.at[0]),
-            pltpu.make_async_copy(all_g.at[0], local_g, kept_sems.at[1]),
-        ]
-        kept_copies = kept_copies or copies
-
-        @pl.when(step == n)
-        def _():
-            for copy in copies:
-                copy.start()
-            local_k[...] = all_k[0]
-            local_run[...] = all_run[0]
-            local_top[...] = all_top[0]
-
+    kept_copies = [
+        pltpu.make_async_copy(all_e.at[step], local_e, kept_sems.at[0]),
+        pltpu.make_async_copy(all_g.at[step], local_g, kept_sems.at[1]),
+    ]
+    for copy in kept_copies:
+        copy.start()
     core, chip = chip_place(index_ref)
 
     def active(j, t):
@@ -279,7 +268,6 @@
             copy.start()
         pl.when(core == 0)(oldest.start)
         pl.when(core == 1)(passed.start)
-        x_acc[...] = jnp.zeros_like(x_acc)
         for copy in copies:
             copy.wait()
         oldest.wait()
@@ -289,9 +277,6 @@
 
     order_pair(q_ref, core, q0, q1)
     order_pair(do_ref, core, do0, do1)
-    gw_acc[...] = jnp.zeros_like(gw_acc)
-    dq_acc[...] = jnp.zeros_like(dq_acc)
-    d_acc[...] = jnp.zeros_like(d_acc)
 
     def lift_block(t):
         def k_out(h, key):
@@ -302,11 +287,11 @@
 
         lift(lat_ref[block_rows(t), :], w_ref, k_out, v_out)
 
-    loop(0, REACH, lambda t: active(0, t) | active(1, t), lift_block)
+    loop(0, REACH, lambda t: active(0, t), lift_block)
 
     for j in range(2):
         for h in range(heads):
-            run_ref[h] = local_run[j * heads + h]
+            run_ref[h] = local_run[0, j * heads + h]
 
         def first_pass(t):
             def keep(h, part, cols, weights, grads):
@@ -329,13 +314,10 @@
             end_ref[h, 2:3, :] = run_ref[h, 2:3, :] * inverse
         q_t, do_t = q_ref[j].T, do_ref[j].T
 
-        def add(t, part, kept, key, top):
-            def r_add(rope):
-                x_acc[LATENT:, part] += rope
-
+        def add(t, kept, key, top, first_q, first_k):
             grad_block(
                 kept, key, top, end_ref, q_t, do_t, low_ref, ds_ref, dq_acc.at[j], d_acc.at[t],
-                r_add,
+                r_acc.at[t], first_q, first_k,
             )
 
         def second_pass(t):
@@ -343,32 +325,57 @@
                 return e_ref[h, piece_rows(t, part), cols], g_ref[h, piece_rows(t, part), cols]
 
             add(
-                t, block_rows(t), kept, lambda h: k_ref[h, block_rows(t), :],
-                lambda h: top_ref[h, t, 0:1, :],
+                t, kept, lambda h: k_ref[h, block_rows(t), :], lambda h: top_ref[h, t, 0:1, :],
+                False, j == 0,
             )
 
-        loop(j, REACH, lambda t: active(j, t), second_pass)
         if j == 0:
             for copy in kept_copies:
                 copy.wait()
+        first_q = True
         for n, (query, t) in enumerate(LOCAL):
             if query == j:
                 add(
-                    t, slice(t * rows, (t + 1) * rows),
+                    t,
                     lambda h, part, cols: (
                         local_e[n * heads + h, part, cols], local_g[n * heads + h, part, cols]
                     ),
-                    lambda h: local_k[(t - REACH) * heads + h],
-                    lambda h: local_top[n * heads + h, 0:1, :],
+                    lambda h: local_k[0, (t - REACH) * heads + h],
+                    lambda h: local_top[0, n * heads + h, 0:1, :],
+                    first_q, t == REACH + j,
                 )
-
-    def project(t):
+                first_q = False
+        loop(j, REACH, lambda t: active(j, t), second_pass)
+
+    def seen(t):
+        return (t >= REACH) | active(0, t)
+
+    def project(t, first):
         part = block_rows(t)
         grads = d_acc[t].astype(jnp.bfloat16)
-        x_acc[:LATENT, part] += dot(w_ref[...], grads)
-        gw_acc[...] += dot(lat_t_ref[:LATENT, part], grads, NT)
-
-    loop(0, blocks, lambda t: (t >= REACH) | active(0, t) | active(1, t), project)
+        weight_part = dot(lat_t_ref[:LATENT, part], grads, NT)
+        gw_acc[...] = weight_part if first else gw_acc[...] + weight_part
+        latent_part = dot(w_ref[...], grads)
+
+        @pl.when(step == 0)
+        def _():
+            x_acc[:LATENT, part] = latent_part
+            x_acc[LATENT:, part] = r_acc[t]
+
+        @pl.when(step > 0)
+        def _():
+            x_acc[:LATENT, part] += latent_part
+            x_acc[LATENT:, part] += r_acc[t]
+
+    @pl.when(step == 0)
+    def _():
+        def clear(t):
+            x_acc[:, block_rows(t)] = jnp.zeros((WIDTH, rows), jnp.float32)
+
+        loop(0, REACH, lambda t: ~seen(t), clear)
+
+    project(REACH, True)
+    loop(0, blocks, lambda t: seen(t) & (t != REACH), lambda t: project(t, False))
     dq0_ref[...] = (dq_acc[core] * SCALE).T.astype(dq0_ref.dtype)
     dq1_ref[...] = (dq_acc[1 - core] * SCALE).T.astype(dq1_ref.dtype)
 
@@ -439,12 +446,12 @@
     )
 
 
-def head_specs(rows, heads, steps, first, in_place):
+def head_specs(rows, heads, steps, in_place):
     def received(i, core):
-        return first + i
+        return i
 
     def own(i, core):
-        return (core * steps if in_place else 0) + first + i
+        return core * steps + i if in_place else i
 
     return [
         core_cols(rows, heads * QK, own), core_cols(rows, heads * VDIM, own),
@@ -453,24 +460,24 @@
     ]
 
 
-def local_scores(index, docs, inputs, latents, heads, steps, step, in_place):
+def local_scores(index, docs, inputs, latents, heads, steps, in_place):
     rows = inputs[0].shape[0]
     low, full = jnp.bfloat16, jnp.float32
     count = len(LOCAL) * heads
     return call(
         local_kernel,
-        1,
-        2 * heads * rows * rows * (3 * (QK + VDIM) + 2 * KV),
+        steps,
+        2 * steps * heads * rows * rows * (3 * (QK + VDIM) + 2 * KV),
         [
-            fixed(1, docs.shape[1]), *head_specs(rows, heads, steps, step, in_place),
+            fixed(1, docs.shape[1]), *head_specs(rows, heads, steps, in_place),
             fixed(WIDTH, rows), fixed(WIDTH, rows),
         ],
         [
-            (step_block(count, rows, rows), (1, count, rows, rows), low),
-            (step_block(count, rows, rows), (1, count, rows, rows), low),
-            (step_block(2 * heads, rows, QK), (1, 2 * heads, rows, QK), low),
-            (step_block(2 * heads, 8, rows), (1, 2 * heads, 8, rows), full),
-            (step_block(count, 8, rows), (1, count, 8, rows), full),
+            (step_block(count, rows, rows), (steps, count, rows, rows), low),
+            (step_block(count, rows, rows), (steps, count, rows, rows), low),
+            (step_block(2 * heads, rows, QK), (steps, 2 * heads, rows, QK), low),
+            (step_block(2 * heads, 8, rows), (steps, 2 * heads, 8, rows), full),
+            (step_block(count, 8, rows), (steps, count, 8, rows), full),
             (fixed(2, 8, rows), (2, 8, rows), jnp.int32),
         ],
         [
@@ -485,25 +492,22 @@
     )(index, docs, *inputs, *latents)
 
 
-def attention(index, doc_ids, inputs, kept, starts, latents, heads, steps, ranks, in_place):
+def attention(index, doc_ids, inputs, kept, latents, heads, steps, ranks, in_place):
     rows = inputs[0].shape[0]
     low, full = jnp.bfloat16, jnp.float32
     count = len(LOCAL) * heads
     window = (REACH + 2) * rows
     far = REACH * rows
     half = (LATENT // 2, steps * heads * KV)
-    every = [entry for part in kept for entry in part]
     return call(
-        functools.partial(main_kernel, ranks, steps),
+        functools.partial(main_kernel, ranks),
         steps,
         2 * steps * heads * rows * rows * (5 * (QK + VDIM) + 8 * (2 * QK + VDIM) + 13 * KV),
-        [SCALARS, *head_specs(rows, heads, steps, 0, in_place)]
-        + [
-            ANYWHERE, ANYWHERE, fixed(1, 2 * heads, rows, QK), fixed(1, 2 * heads, 8, rows),
-            fixed(1, count, 8, rows),
+        [
+            SCALARS, *head_specs(rows, heads, steps, in_place), ANYWHERE, ANYWHERE,
+            step_block(2 * heads, rows, QK), step_block(2 * heads, 8, rows),
+            step_block(count, 8, rows), fixed(2, 8, rows),
         ]
-        * steps
-        + [fixed(2, 8, rows)]
         + [ANYWHERE] * len(latents),
         [(step_cols(rows, heads * QK), (rows, steps * heads * QK), low)] * 2
         + [(step_cols(LATENT // 2, heads * KV), half, low)] * 2
@@ -528,16 +532,14 @@
             ((REACH + 2, heads * KV, rows), full),
             ((LATENT, heads * KV), full),
             ((WIDTH, window), full),
+            ((REACH + 2, ROPE, rows), full),
             ((count, rows, rows), low),
             ((count, rows, rows), low),
-            ((2 * heads, rows, QK), low),
-            ((2 * heads, 8, rows), full),
-            ((count, 8, rows), full),
             pltpu.SemaphoreType.DMA((5,)),
             pltpu.SemaphoreType.DMA((2,)),
         ],
         "attention",
-    )(index, doc_ids, *inputs, *every, starts, *latents)
+    )(index, doc_ids, *inputs, *kept, *latents)
 
 
 def permute(value, axis, target):
@@ -575,19 +577,13 @@
         across(own_heads(grad_out, 1 - core)),
         kv_up_weight if in_place else own_heads(kv_up_weight, core),
     )
-    kept = []
-    for step in range(steps):
-        *parts, starts = local_scores(
-            index, docs, inputs, (latent, other), heads, steps, step, in_place
-        )
-        kept.append(parts)
-        if step == 0:
-            far, mixed, parts[-1] = lax.optimization_barrier((far, mixed, parts[-1]))
-            swapped = across(far)
-            passed = permute(mixed, "ctx", lambda s: -1 if s % 2 else s + 1)
+    *kept, starts = local_scores(index, docs, inputs, (latent, other), heads, steps, in_place)
+    far, mixed, starts = lax.optimization_barrier((far, mixed, starts))
+    swapped = across(far)
+    passed = permute(mixed, "ctx", lambda s: -1 if s % 2 else s + 1)
 
     dq_own, dq_other, keep, send, to_old, to_far, to_swap, mine, to_other = attention(
-        index, doc_ids, inputs, kept, starts,
+        index, doc_ids, inputs, (*kept, starts),
         (far, swapped, mixed, passed, latent, other), heads, steps, ranks, in_place,
     )
 

time: 143 us -> 133 us (0.930)
  the two profiles are of different devices: /device:TPU:10 before, /device:TPU:0 now
where the time goes in v1:
time: 133 us; the launch traced here: 131 us
  starting transfers between devices  49.4 us (37%)
  Pallas kernels  39.3 us (30%)
  waiting for transfers between devices  24.2 us (18%)
  other arithmetic  13.3 us (10%)
  local copies, waits for them, and re-layouts  4.12 us (3%)
    pallas_call x1, Pallas kernels, attention(): call(functools.partial(main_kernel, ranks), steps, 2 * steps * heads * ro...  25.9 us
    ppermute x15, starting transfers between devices, permute(): return lax.ppermute(value, axis, pairs)  25.4 us
    all_to_all x1, starting transfers between devices, local(): lax.all_to_all(plane, 'ctx', 0, 0, axis_index_groups=columns, tiled=True)  22.4 us
    all_to_all x1, waiting for transfers between devices, local(): lax.all_to_all(plane, 'ctx', 0, 0, axis_index_groups=columns, tiled=True)  15.4 us
    pallas_call x1, Pallas kernels, local_scores(): call(local_kernel, steps, 2 * steps * heads * rows * rows * (3 * (QK + VD...  13.4 us
    ppermute x15, waiting for transfers between devices, permute(): return lax.ppermute(value, axis, pairs)  8.75 us
    unnamed x24, local copies, waits for them, and re-layouts  2.76 us
  transfers between devices with their start and end apart: 17, of which 4 were waited for; matrix products, arithmetic and copies ran while one was open for 8% of the time, Pallas kernels for 10%

profile of v1, /device:TPU:0, one launch (start us, length us, event | category | flops | bytes accessed | tf_op | source)
XLA Modules:
  0.0 131.2 jit_solution(8418476838332489424)
XLA Ops:
  0.6 0.0 copy-start.4
  0.6 0.0 copy-start.6
  0.7 1.3 constant_dynamic-slice_fusion.2
  2.0 0.5 collective-permute-start
  2.5 0.1 collective-permute-start.2
  2.6 0.5 collective-permute-start.1
  3.1 4.5 %collective-permute-start.3 = (bf16[576,512]{1,0:T(8,128)(2,1)S(1)}, bf16[576,512]{1,0:T(8,128)(2,1)S(1)}, u32[]{:S(2)}, u32[]{:S(2)}) collective-permute-start(bf16[576,512]{1,0:T(8,128)(2,1)S(1)} %bitcast.9), channel_id=1, source_target_pairs={{0,4},{2,6},{4,8},{6,10},{8,12},{10,14},{12,16},{14,18},{16,20},{1... | collective-permute-start | bytes 1769480 | tf_op jit(solution)/shard_map/ppermute | solution.py:548
  7.6 0.7 collective-permute-start.4
  8.3 0.0 collective-permute-done.1.do1
  8.3 0.0 collective-permute-done.q1
  8.4 0.0 copy-start.5
  8.4 0.8 copy-done.11
  9.1 0.3 copy-done.5
  9.4 13.4 %local_scores.1 = (bf16[2,6,512,512]{3,2,1,0:T(8,128)(2,1)}, bf16[2,6,512,512]{3,2,1,0:T(8,128)(2,1)}, bf16[2,4,512,192]{3,2,1,0:T(8,128)(2,1)}, f32[2,4,8,512]{...) custom-call(s32[1]{0:T(128)} %bitcast.index_ref, s32[1,8192]{1,0:T(1,128)} %bitcast.11, ...), custom_call_target="tpu_custom_call" | custom-call | flops 3087007744 | bytes 16777216 | tf_op jit(solution)/shard_map/local_scores/pallas_call | solution.py:467
  22.8 0.0 collective-permute-done.3.lat_far
  22.8 0.0 copy-start.7
  22.8 3.0 %collective-permute-start.5 = (bf16[576,512]{1,0:T(8,128)(2,1)S(1)}, bf16[576,512]{1,0:T(8,128)(2,1)S(1)}, u32[]{:S(2)}, u32[]{:S(2)}) collective-permute-start(bf16[576,512]{1,0:T(8,128)(2,1)S(1)} %collective-permute-done.3.lat_far), channel_id=1, source_target_pairs={{0,2},{2,0},{4,6},{6,4},{8,10},{10,8},{12,14},{14,12},{16,18},{18,... | collective-permute-start | bytes 1769480 | tf_op jit(solution)/shard_map/ppermute | solution.py:548
  25.8 2.1 %collective-permute-start.6 = (bf16[576,512]{1,0:T(8,128)(2,1)S(1)}, bf16[576,512]{1,0:T(8,128)(2,1)S(1)}, u32[]{:S(2)}, u32[]{:S(2)}) collective-permute-start(bf16[576,512]{1,0:T(8,128)(2,1)S(1)} %collective-permute-done.4.lat_mixed), channel_id=1, source_target_pairs={{0,2},{4,6},{8,10},{12,14},{16,18},{20,22},{24,26},{28,30},{1,3},{... | collective-permute-start | bytes 1769480 | tf_op jit(solution)/shard_map/ppermute | solution.py:548
  27.9 0.0 collective-permute-done.5.lat_swap
  28.0 1.4 %collective-permute-done.6.lat_passed = bf16[576,512]{1,0:T(8,128)(2,1)S(1)} collective-permute-done((bf16[576,512]{1,0:T(8,128)(2,1)S(1)}, bf16[576,512]{1,0:T(8,128)(2,1)S(1)}, u32[]{:S(2)}, u32[]{:S(2)}) %collective-permute-start.6) | collective-permute-done | bytes 589856 | tf_op jit(solution)/shard_map/ppermute | solution.py:548
  29.3 0.8 copy-done.10
  30.2 25.9 %attention.1 = (bf16[512,768]{1,0:T(8,128)(2,1)}, bf16[512,768]{1,0:T(8,128)(2,1)}, bf16[256,1024]{1,0:T(8,128)(2,1)}, bf16[256,1024]{1,0:T(8,128)(2,1)}, bf16[5...) custom-call(s32[1]{0:T(128)} %bitcast.index_ref, ...), custom_call_target="tpu_custom_call" | custom-call | flops 18924699648 | bytes 16777216 | tf_op jit(solution)/shard_map/attention/pallas_call | solution.py:502
  56.1 1.4 %collective-permute-start.9 = (bf16[576,512]{1,0:T(8,128)(2,1)}, bf16[576,512]{1,0:T(8,128)(2,1)S(1)}, u32[]{:S(2)}, u32[]{:S(2)}) collective-permute-start(bf16[576,512]{1,0:T(8,128)(2,1)} %get-tuple-element.35), channel_id=1, source_target_pairs={{2,0},{6,4},{10,8},{14,12},{18,16},{22,20},{26,24},{30,28},{3,1},{... | collective-permute-start | bytes 1769480 | tf_op jit(solution)/shard_map/ppermute | solution.py:548
  57.5 1.2 collective-permute-start.11
  58.8 8.7 %collective-permute-start.14 = (bf16[256,1024]{1,0:T(8,128)(2,1)}, bf16[256,1024]{1,0:T(8,128)(2,1)S(1)}, u32[]{:S(2)}, u32[]{:S(2)}) collective-permute-start(bf16[256,1024]{1,0:T(8,128)(2,1)} %get-tuple-element.39), channel_id=1, source_target_pairs={{0,4},{2,6},{4,0},{6,2},{8,12},{10,14},{12,8},{14,10},{16,20},{18,... | collective-permute-start | bytes 1572872 | tf_op jit(solution)/shard_map/ppermute | solution.py:548
  67.5 0.0 collective-permute-start.8
  67.5 0.5 collective-permute-start.7
  68.0 2.0 %add_convert_fusion.2 = bf16[576,512]{1,0:T(8,128)(2,1)} fusion(bf16[576,512]{1,0:T(8,128)(2,1)S(1)} %collective-permute-done.9, bf16[576,512]{1,0:T(8,128)(2,1)} %get-tuple-element.35), kind=kLoop, calls=%fused_computation.4 | loop fusion | flops 1179648 | bytes 1769472 | tf_op jit(solution)/shard_map/convert_element_type | solution.py:595
  70.1 0.8 collective-permute-start.10
  70.9 1.0 add_convert_fusion.1
  71.9 1.3 collective-permute-start.12
  73.2 7.3 %collective-permute-done.14 = bf16[256,1024]{1,0:T(8,128)(2,1)S(1)} collective-permute-done((bf16[256,1024]{1,0:T(8,128)(2,1)}, bf16[256,1024]{1,0:T(8,128)(2,1)S(1)}, u32[]{:S(2)}, u32[]{:S(2)}) %collective-permute-start.14) | collective-permute-done | bytes 524320 | tf_op jit(solution)/shard_map/ppermute | solution.py:548
  80.4 1.0 add_convert_fusion.3
  81.4 22.4 %all-to-all-start = ((bf16[4,64,1024]{2,1,0:T(8,128)(2,1)}), bf16[4,64,1024]{2,1,0:T(8,128)(2,1)}, u32[]{:S(2)}, u32[]{:S(2)}) async-start(bf16[4,64,1024]{2,1,0:T(8,128)(2,1)} %bitcast.4), calls=%async_computation | async-start | bytes 1048576 | tf_op jit(solution)/shard_map/all_to_all | solution.py:601
  103.8 0.0 collective-permute-done.7
  103.8 0.9 copy-done.1
  104.7 1.5 %broadcast_select_fusion.1 = (bf16[512,768]{1,0:T(8,128)(2,1)S(1)}, bf16[512,768]{1,0:T(8,128)(2,1)S(1)}) fusion(bf16[512,768]{1,0:T(8,128)(2,1)} %get-tuple-element.31, bf16[512,768]{1,0:T(8,128)(2,1)} %copy-done.1, pred[]{:T(512)S(6)} %eq.2), kind=kLoop, calls=%fused_computation.8 | loop fusion | flops 786432 | bytes 3145729 | tf_op jit(solution)/shard_map/jit(_where)/select_n | solution.py:606
  106.3 0.0 collective-permute-done.10
  106.3 0.0 collective-permute-done.12
  106.3 2.2 %fusion.1 = bf16[576,512]{1,0:T(8,128)(2,1)} fusion(bf16[576,512]{1,0:T(8,128)(2,1)} %collective-permute-done.12, bf16[576,512]{1,0:T(8,128)(2,1)S(1)} %collective-permute-done.10, bf16[576,512]{1,0:T(8,128)(2,1)S(1)} %collective-permute-done.8, bf16[576,512]{1,0:T(8,128)(2,1)S(1)} %copy-done), kind=kLoop, calls=%fused_computation.10 | loop fusion | flops 2359296 | bytes 2949120 | tf_op jit(solution)/shard_map/convert_element_type | solution.py:617
  108.5 1.5 %collective-permute-start.13 = (bf16[576,512]{1,0:T(8,128)(2,1)}, bf16[576,512]{1,0:T(8,128)(2,1)}, u32[]{:S(2)}, u32[]{:S(2)}) collective-permute-start(bf16[576,512]{1,0:T(8,128)(2,1)} %fusion.1), channel_id=1, source_target_pairs={{0,1},{1,0},{2,3},{3,2},{4,5},{5,4},{6,7},{7,6},{8,9},{9,8},{10,11... | collective-permute-start | bytes 1769480 | tf_op jit(solution)/shard_map/ppermute | solution.py:620
  110.0 15.4 %all-to-all-done = bf16[4,64,1024]{2,1,0:T(8,128)(2,1)} async-done(((bf16[4,64,1024]{2,1,0:T(8,128)(2,1)}), bf16[4,64,1024]{2,1,0:T(8,128)(2,1)}, u32[]{:S(2)}, u32[]{:S(2)}) %all-to-all-start) | async-done | bytes 524320 | tf_op jit(solution)/shard_map/all_to_all | solution.py:601
  125.4 1.1 convert_reduce_fusion
  126.6 0.1 collective-permute-start.15
  126.7 1.3 pad_maximum_fusion
  127.9 0.1 collective-permute-done.15
  128.0 0.7 pad_maximum_fusion.1
  128.8 2.4 %fusion = bf16[512,576]{0,1:T(8,128)(2,1)} fusion(bf16[576,512]{1,0:T(8,128)(2,1)} %collective-permute-done.13, bf16[576,512]{1,0:T(8,128)(2,1)} %collective-permute-done.12, bf16[576,512]{1,0:T(8,128)(2,1)S(1)} %collective-permute-done.10, bf16[576,512]{1,0:T(8,128)(2,1)S(1)} %collective-permute-done.8, bf16[576,512]{1,0:T(8,128)(2,1)S(1)} %copy-done), kind=kLoop, calls=%fused_computation.9 | loop fusion | flops 2949120 | bytes 3538944 | tf_op jit(solution)/shard_map/transpose | solution.py:622
  (25 shorter events, 0.1 us)
Async XLA Ops:
  0.6 1.9 %copy-start.4 = (bf16[512,1024]{1,0:T(8,128)(2,1)S(1)}, bf16[512,1024]{1,0:T(8,128)(2,1)}, u32[]{:S(2)}) copy-start(bf16[512,1024]{1,0:T(8,128)(2,1)} %do0.3) | copy-start | bytes 3145732
  0.6 2.5 %copy-start.6 = (bf16[512,576]{0,1:T(8,128)(2,1)S(1)}, bf16[512,576]{0,1:T(8,128)(2,1)}, u32[]{:S(2)}) copy-start(bf16[512,576]{0,1:T(8,128)(2,1)} %param.5) | copy-start | bytes 1769476
  2.0 6.4 %collective-permute-start = (bf16[512,768]{1,0:T(8,128)(2,1)S(1)}, bf16[512,768]{1,0:T(8,128)(2,1)S(1)}, u32[]{:S(2)}, u32[]{:S(2)}) collective-permute-start(bf16[512,768]{1,0:T(8,128)(2,1)S(1)} %constant_dynamic-slice_fusion.2), channel_id=1, source_target_pairs={{0,2},{2,0},{4,6},{6,4},{8,10},{10,8},{12,14},{14,12},{16,18},{18,... | collective-permute-start | bytes 2359304 | tf_op jit(solution)/shard_map/ppermute | solution.py:548
  2.5 5.9 %collective-permute-start.2 = (bf16[576,512]{1,0:T(8,128)(2,1)}, bf16[576,512]{1,0:T(8,128)(2,1)}, u32[]{:S(2)}, u32[]{:S(2)}) collective-permute-start(bf16[576,512]{1,0:T(8,128)(2,1)} %bitcast.6), channel_id=1, source_target_pairs={{0,2},{2,0},{4,6},{6,4},{8,10},{10,8},{12,14},{14,12},{16,18},{18,... | collective-permute-start | bytes 1769480 | tf_op jit(solution)/shard_map/ppermute | solution.py:548
  2.6 5.7 %collective-permute-start.1 = (bf16[512,512]{1,0:T(8,128)(2,1)S(1)}, bf16[512,512]{1,0:T(8,128)(2,1)S(1)}, u32[]{:S(2)}, u32[]{:S(2)}) collective-permute-start(bf16[512,512]{1,0:T(8,128)(2,1)S(1)} %constant_dynamic-slice_fusion.1), channel_id=1, source_target_pairs={{0,2},{2,0},{4,6},{6,4},{8,10},{10,8},{12,14},{14,12},{16,18},{18,... | collective-permute-start | bytes 1572872 | tf_op jit(solution)/shard_map/ppermute | solution.py:548
  3.1 19.7 %collective-permute-start.3 = (bf16[576,512]{1,0:T(8,128)(2,1)S(1)}, bf16[576,512]{1,0:T(8,128)(2,1)S(1)}, u32[]{:S(2)}, u32[]{:S(2)}) collective-permute-start(bf16[576,512]{1,0:T(8,128)(2,1)S(1)} %bitcast.9), channel_id=1, source_target_pairs={{0,4},{2,6},{4,8},{6,10},{8,12},{10,14},{12,16},{14,18},{16,20},{1... | collective-permute-start | bytes 1769480 | tf_op jit(solution)/shard_map/ppermute | solution.py:548
  7.6 15.2 %collective-permute-start.4 = (bf16[576,512]{1,0:T(8,128)(2,1)S(1)}, bf16[576,512]{1,0:T(8,128)(2,1)S(1)}, u32[]{:S(2)}, u32[]{:S(2)}) collective-permute-start(bf16[576,512]{1,0:T(8,128)(2,1)S(1)} %bitcast.10), channel_id=1, source_target_pairs={{2,8},{6,12},{10,16},{14,20},{18,24},{22,28},{3,9},{7,13},{11,17},... | collective-permute-start | bytes 1769480 | tf_op jit(solution)/shard_map/ppermute | solution.py:548
  8.3 0.8 copy-start.11
  8.4 1.0 copy-start.5
  22.8 6.5 %copy-start.7 = (bf16[576,512]{1,0:T(8,128)(2,1)}, bf16[576,512]{1,0:T(8,128)(2,1)S(1)}, u32[]{:S(2)}) copy-start(bf16[576,512]{1,0:T(8,128)(2,1)S(1)} %collective-permute-done.3.lat_far) | copy-start | bytes 1769476
  22.8 6.5 %copy-start.8 = (bf16[576,512]{1,0:T(8,128)(2,1)}, bf16[576,512]{1,0:T(8,128)(2,1)S(1)}, u32[]{:S(2)}) copy-start(bf16[576,512]{1,0:T(8,128)(2,1)S(1)} %collective-permute-done.4.lat_mixed) | copy-start | bytes 1769476
  22.8 5.1 %collective-permute-start.5 = (bf16[576,512]{1,0:T(8,128)(2,1)S(1)}, bf16[576,512]{1,0:T(8,128)(2,1)S(1)}, u32[]{:S(2)}, u32[]{:S(2)}) collective-permute-start(bf16[576,512]{1,0:T(8,128)(2,1)S(1)} %collective-permute-done.3.lat_far), channel_id=1, source_target_pairs={{0,2},{2,0},{4,6},{6,4},{8,10},{10,8},{12,14},{14,12},{16,18},{18,... | collective-permute-start | bytes 1769480 | tf_op jit(solution)/shard_map/ppermute | solution.py:548
  25.8 3.5 %collective-permute-start.6 = (bf16[576,512]{1,0:T(8,128)(2,1)S(1)}, bf16[576,512]{1,0:T(8,128)(2,1)S(1)}, u32[]{:S(2)}, u32[]{:S(2)}) collective-permute-start(bf16[576,512]{1,0:T(8,128)(2,1)S(1)} %collective-permute-done.4.lat_mixed), channel_id=1, source_target_pairs={{0,2},{4,6},{8,10},{12,14},{16,18},{20,22},{24,26},{28,30},{1,3},{... | collective-permute-start | bytes 1769480 | tf_op jit(solution)/shard_map/ppermute | solution.py:548
  27.9 1.4 %copy-start.9 = (bf16[576,512]{1,0:T(8,128)(2,1)}, bf16[576,512]{1,0:T(8,128)(2,1)S(1)}, u32[]{:S(2)}) copy-start(bf16[576,512]{1,0:T(8,128)(2,1)S(1)} %collective-permute-done.5.lat_swap) | copy-start | bytes 1769476
  29.3 0.8 copy-start.10
  56.1 14.8 %copy-start.2 = (bf16[576,512]{1,0:T(8,128)(2,1)S(1)}, bf16[576,512]{1,0:T(8,128)(2,1)}, u32[]{:S(2)}) copy-start(bf16[576,512]{1,0:T(8,128)(2,1)} %get-tuple-element.36) | copy-start | bytes 1769476
  56.1 11.9 %collective-permute-start.9 = (bf16[576,512]{1,0:T(8,128)(2,1)}, bf16[576,512]{1,0:T(8,128)(2,1)S(1)}, u32[]{:S(2)}, u32[]{:S(2)}) collective-permute-start(bf16[576,512]{1,0:T(8,128)(2,1)} %get-tuple-element.35), channel_id=1, source_target_pairs={{2,0},{6,4},{10,8},{14,12},{18,16},{22,20},{26,24},{30,28},{3,1},{... | collective-permute-start | bytes 1769480 | tf_op jit(solution)/shard_map/ppermute | solution.py:548
  57.5 13.3 %collective-permute-start.11 = (bf16[576,512]{1,0:T(8,128)(2,1)}, bf16[576,512]{1,0:T(8,128)(2,1)S(1)}, u32[]{:S(2)}, u32[]{:S(2)}) collective-permute-start(bf16[576,512]{1,0:T(8,128)(2,1)} %get-tuple-element.37), channel_id=1, source_target_pairs={{0,2},{2,0},{4,6},{6,4},{8,10},{10,8},{12,14},{14,12},{16,18},{18,... | collective-permute-start | bytes 1769480 | tf_op jit(solution)/shard_map/ppermute | solution.py:548
  58.8 21.7 %collective-permute-start.14 = (bf16[256,1024]{1,0:T(8,128)(2,1)}, bf16[256,1024]{1,0:T(8,128)(2,1)S(1)}, u32[]{:S(2)}, u32[]{:S(2)}) collective-permute-start(bf16[256,1024]{1,0:T(8,128)(2,1)} %get-tuple-element.39), channel_id=1, source_target_pairs={{0,4},{2,6},{4,0},{6,2},{8,12},{10,14},{12,8},{14,10},{16,20},{18,... | collective-permute-start | bytes 1572872 | tf_op jit(solution)/shard_map/ppermute | solution.py:548
  67.5 38.8 %collective-permute-start.8 = (bf16[576,512]{1,0:T(8,128)(2,1)}, bf16[576,512]{1,0:T(8,128)(2,1)S(1)}, u32[]{:S(2)}, u32[]{:S(2)}) collective-permute-start(bf16[576,512]{1,0:T(8,128)(2,1)} %get-tuple-element.34), channel_id=1, source_target_pairs={{0,2},{2,0},{4,6},{6,4},{8,10},{10,8},{12,14},{14,12},{16,18},{18,... | collective-permute-start | bytes 1769480 | tf_op jit(solution)/shard_map/ppermute | solution.py:548
  67.5 36.3 %collective-permute-start.7 = (bf16[512,768]{1,0:T(8,128)(2,1)}, bf16[512,768]{1,0:T(8,128)(2,1)S(1)}, u32[]{:S(2)}, u32[]{:S(2)}) collective-permute-start(bf16[512,768]{1,0:T(8,128)(2,1)} %get-tuple-element.32), channel_id=1, source_target_pairs={{0,2},{2,0},{4,6},{6,4},{8,10},{10,8},{12,14},{14,12},{16,18},{18,... | collective-permute-start | bytes 2359304 | tf_op jit(solution)/shard_map/ppermute | solution.py:548
  70.0 10.4 %copy-start.3 = (bf16[256,1024]{1,0:T(8,128)(2,1)S(1)}, bf16[256,1024]{1,0:T(8,128)(2,1)}, u32[]{:S(2)}) copy-start(bf16[256,1024]{1,0:T(8,128)(2,1)} %get-tuple-element.38) | copy-start | bytes 1572868
  70.1 36.2 %collective-permute-start.10 = (bf16[576,512]{1,0:T(8,128)(2,1)}, bf16[576,512]{1,0:T(8,128)(2,1)S(1)}, u32[]{:S(2)}, u32[]{:S(2)}) collective-permute-start(bf16[576,512]{1,0:T(8,128)(2,1)} %add_convert_fusion.2), channel_id=1, source_target_pairs={{8,2},{12,6},{16,10},{20,14},{24,18},{28,22},{9,3},{13,7},{17,11},... | collective-permute-start | bytes 1769480 | tf_op jit(solution)/shard_map/ppermute | solution.py:548
  71.9 34.4 %collective-permute-start.12 = (bf16[576,512]{1,0:T(8,128)(2,1)}, bf16[576,512]{1,0:T(8,128)(2,1)}, u32[]{:S(2)}, u32[]{:S(2)}) collective-permute-start(bf16[576,512]{1,0:T(8,128)(2,1)} %add_convert_fusion.1), channel_id=1, source_target_pairs={{4,0},{6,2},{8,4},{10,6},{12,8},{14,10},{16,12},{18,14},{20,16},{2... | collective-permute-start | bytes 1769480 | tf_op jit(solution)/shard_map/ppermute | solution.py:548
  81.4 44.0 %all-to-all-start = ((bf16[4,64,1024]{2,1,0:T(8,128)(2,1)}), bf16[4,64,1024]{2,1,0:T(8,128)(2,1)}, u32[]{:S(2)}, u32[]{:S(2)}) async-start(bf16[4,64,1024]{2,1,0:T(8,128)(2,1)} %bitcast.4), calls=%async_computation | async-start | bytes 1048576 | tf_op jit(solution)/shard_map/all_to_all | solution.py:601
  103.8 0.9 copy-start.1
  104.7 1.6 %copy-start = (bf16[576,512]{1,0:T(8,128)(2,1)S(1)}, bf16[576,512]{1,0:T(8,128)(2,1)}, u32[]{:S(2)}) copy-start(bf16[576,512]{1,0:T(8,128)(2,1)} %get-tuple-element.33) | copy-start | bytes 1769476
  108.5 20.3 %collective-permute-start.13 = (bf16[576,512]{1,0:T(8,128)(2,1)}, bf16[576,512]{1,0:T(8,128)(2,1)}, u32[]{:S(2)}, u32[]{:S(2)}) collective-permute-start(bf16[576,512]{1,0:T(8,128)(2,1)} %fusion.1), channel_id=1, source_target_pairs={{0,1},{1,0},{2,3},{3,2},{4,5},{5,4},{6,7},{7,6},{8,9},{9,8},{10,11... | collective-permute-start | bytes 1769480 | tf_op jit(solution)/shard_map/ppermute | solution.py:620
  126.6 1.4 %collective-permute-start.15 = (f32[32,1024]{1,0:T(8,128)S(1)}, f32[32,1024]{1,0:T(8,128)S(1)}, u32[]{:S(2)}, u32[]{:S(2)}) collective-permute-start(f32[32,1024]{1,0:T(8,128)S(1)} %constant_dynamic-slice_fusion), channel_id=1, source_target_pairs={{0,2},{2,0},{4,6},{6,4},{8,10},{10,8},{12,14},{14,12},{16,18},{18,... | collective-permute-start | bytes 393224 | tf_op jit(solution)/shard_map/ppermute | solution.py:548
